TPU v7x, 32 devices: a whole 2x2x4 slice. The times are simulated.
32 devices in a mesh: row: 8 (over y, x, core), col: 4 (over z).
Axes of the slice: x: 2, y: 2, z: 4, core: 2. Of those that a mesh axis runs over, the one named last changes fastest.
Arguments:
- affiliation: bfloat16 [16384, 512], P(('row', 'col'))
- wanted_tiles: int32 [4, 8, 8], P('col', None, 'row'), may hold values from 0 to 3
- slot_peers: int32 [4, 8, 128], P('col', None, 'row'), may hold values from 0 to 7, as said below
- edge_words: int32 [4, 8, 16, 16384], P('col', None, None, 'row'), may hold values from 0 to 255, as said below
Outputs:
- affiliation_next: float32 [16384, 512], P(('row', 'col'))
Inputs may be any that keep to these rules, and one draw needn't show every extreme that they name: `slot_peers`: the 8 entries of one column group and one row tile are distinct. `edge_words`: each word holds 8 mask bits.
All inputs are finite; a program needn't handle non-finite values.
Results may differ from a plain program's by a relative error of at most 0.0003.
Values may be sent and summed in bfloat16 or wider, within the bound.
A program may use at most 128 MiB of HBM per device.

v0:
```python
import math

import jax
import jax.numpy as jnp
from jax import lax
from jax.sharding import PartitionSpec as P

TILE = 128
NBR = 8


BACKGROUND = 0.25
NEG_RATE = 0.1
STEP_SIZE = 0.005


def unpack(mask_words):
    shifts = jnp.arange(8, dtype=jnp.int32)
    arc_bits = jnp.bitwise_and(jnp.right_shift(mask_words[..., :, None, :], shifts[:, None]), 1)
    return arc_bits.reshape(
        mask_words.shape[:-2] + (mask_words.shape[-2] * 8, mask_words.shape[-1])
    )


def local(affiliation, wanted_tiles, slot_peers, edge_words):
    own_rows, community = affiliation.shape
    rows_axis = lax.axis_size("row")
    cols_axis = lax.axis_size("col")
    node_count = own_rows * rows_axis * cols_axis
    neg_weight = NEG_RATE * NBR * TILE / node_count
    own_tiles = own_rows // TILE
    range_rows = lax.all_gather(affiliation, "col", axis=0, tiled=True)
    requests = wanted_tiles.reshape(rows_axis)
    group_rows = lax.all_gather(affiliation, "row", axis=0, tiled=True)
    fetched = group_rows.reshape(rows_axis, own_tiles, TILE, community)[
        jnp.arange(rows_axis), requests
    ]
    column_sums = lax.psum(jnp.sum(affiliation, axis=0, dtype=jnp.float32), ("row", "col"))
    peer_table = slot_peers.reshape(NBR, -1)
    word_table = edge_words.reshape(NBR, TILE // 8, -1)
    row_tiles = range_rows.reshape(-1, TILE, community)
    row_count = own_rows * lax.axis_size("col")
    block_tiles = math.gcd(4, row_count // TILE)

    def one_block(block_index):
        start_tile = block_index * block_tiles
        row_block = lax.dynamic_slice_in_dim(row_tiles, start_tile, block_tiles, 0)
        peer_ids = lax.dynamic_slice_in_dim(peer_table, start_tile, block_tiles, 1)
        col_block = fetched[peer_ids]
        mask_words = lax.dynamic_slice_in_dim(word_table, start_tile * TILE, block_tiles * TILE, 2)
        arc_bits = unpack(mask_words).reshape(NBR, TILE, block_tiles, TILE).astype(jnp.float32)
        scores = (
            jnp.einsum("jbvk,buk->jvbu", col_block, row_block, preferred_element_type=jnp.float32)
            / community
            + BACKGROUND
        )
        weights = (arc_bits * (1.0 / jnp.expm1(scores) + neg_weight)).astype(jnp.bfloat16)
        attract = jnp.einsum(
            "jvbu,jbvk->buk", weights, col_block, preferred_element_type=jnp.float32
        )
        return attract.reshape(block_tiles * TILE, community)

    blocks_out = lax.map(one_block, jnp.arange(row_count // (block_tiles * TILE), dtype=jnp.int32))
    merged = lax.psum_scatter(
        blocks_out.reshape(row_count, community), "col", scatter_dimension=0, tiled=True
    )
    own_values = affiliation.astype(jnp.float32)
    gradient = merged - neg_weight * (column_sums[None, :] - own_values)
    return jnp.maximum(own_values + STEP_SIZE * gradient, 0.0)


def solution(mesh):
    in_specs = (
        P(("row", "col"), None),
        P("col", None, "row"),
        P("col", None, "row"),
        P("col", None, None, "row"),
    )
    out_specs = P(("row", "col"), None)
    return jax.shard_map(local, mesh=mesh, in_specs=in_specs, out_specs=out_specs, check_vma=False)
```

profile of v0, /device:TPU:1, one launch (start us, length us, event | category | flops | bytes accessed | tf_op | source)
XLA Modules:
  0.0 270.7 jit_solution(13263209883986246414)
XLA Ops:
  6.5 0.7 all-gather.5.cloned.1.call-update
  7.3 0.7 all-gather.3.cloned.1.call-update
  8.1 0.7 fusion.18
  8.7 39.8 %all-gather.5.cloned.1.call-done = bf16[4096,512]{1,0:T(8,128)(2,1)} async-done(((bf16[512,512]{1,0:T(8,128)(2,1)}), bf16[4096,512]{1,0:T(8,128)(2,1)}) %all-gather.5.cloned.1.call-update) | async-done | bytes 4194320 | tf_op jit(solution)/shard_map/all_gather | solution.py:34
  48.5 2.8 %gather_fusion.1 = bf16[8,128,512]{2,1,0:T(8,128)(2,1)S(1)} fusion(bf16[8,4,128,512]{3,2,1,0:T(8,128)(2,1)} %bitcast.45, s32[8]{0:T(128)S(1)} %fusion.18), kind=kCustom, calls=%fused_computation.1 | custom fusion | bytes 2097216 | tf_op jit(solution)/shard_map/gather | solution.py:35
  51.3 44.3 %all-gather.3.cloned.1.call-done = bf16[2048,512]{1,0:T(8,128)(2,1)} async-done(((bf16[512,512]{1,0:T(8,128)(2,1)}), bf16[2048,512]{1,0:T(8,128)(2,1)}) %all-gather.3.cloned.1.call-update) | async-done | bytes 2097168 | tf_op jit(solution)/shard_map/all_gather | solution.py:32
  95.6 89.3 %while.12 = (s32[]{:T(128)}, f32[4,512,512]{2,1,0:T(8,128)}, s32[4]{0:T(128)S(1)}, s32[8,16,2048]{2,1,0:T(8,128)}, bf16[16,128,512]{2,1,0:T(8,128)(2,1)}, /*inde...) while((s32[]{:T(128)}, f32[4,512,512]{2,1,0:T(8,128)}, ...), condition=%wide.region_1.0_spmd, body=%wide.region_0.0_spmd.sunk | while | flops 1078461568 | bytes 56892936 | solution.py:63
  95.6 0.6 dynamic_slice.38
  97.0 2.8 %gather_fusion = bf16[32,128,512]{2,1,0:T(8,128)(2,1)} fusion(bf16[8,128,512]{2,1,0:T(8,128)(2,1)S(1)} %get-tuple-element.184, s32[1024]{0:T(1024)S(1)} %pad_clamp_fusion.2), kind=kCustom, calls=%fused_computation.clone.1 | custom fusion | bytes 8388736 | tf_op jit(solution)/shard_map/while/body/eval_jaxpr/gather | solution.py:49
  99.8 5.3 %divide_add_fusion.2 = f32[4,128,8,128]{3,1,2,0:T(8,128)} fusion(bf16[8,4,128,512]{3,2,1,0:T(8,128)(2,1)} %bitcast.41, bf16[16,128,512]{2,1,0:T(8,128)(2,1)} %get-tuple-element.182, s32[]{:T(128)S(6)} %select_n.45), kind=kOutput, calls=%fused_computation.6.clone.1 | convolution fusion | flops 538968064 | bytes 6815748 | tf_op jit(solution)/shard_map/while/body/eval_jaxpr/jbvk,buk->jvbu/dot_general | solution.py:53
  105.0 2.0 copy.27
  107.7 1.0 constant_dynamic-slice_fusion.2
  108.7 1.6 shift_right_arithmetic.33
  110.3 2.9 %shift_right_arithmetic.34 = s32[8,128,4,128]{3,2,1,0:T(4,128)} reshape(s32[8,16,8,512]{3,2,1,0:T(8,128)} %shift_right_arithmetic.33) | data formatting | bytes 4194304 | tf_op jit(solution)/shard_map/while/body/eval_jaxpr/shift_right_arithmetic | solution.py:19
  113.3 2.6 fusion.29
  116.1 0.8 fusion.30
  116.9 1.1 constant_dynamic-update-slice_fusion.2
  119.3 2.8 %gather_fusion = bf16[32,128,512]{2,1,0:T(8,128)(2,1)} fusion(bf16[8,128,512]{2,1,0:T(8,128)(2,1)S(1)} %get-tuple-element.184, s32[1024]{0:T(1024)S(1)} %pad_clamp_fusion.2), kind=kCustom, calls=%fused_computation.clone.1 | custom fusion | bytes 8388736 | tf_op jit(solution)/shard_map/while/body/eval_jaxpr/gather | solution.py:49
  122.1 5.2 %divide_add_fusion.2 = f32[4,128,8,128]{3,1,2,0:T(8,128)} fusion(bf16[8,4,128,512]{3,2,1,0:T(8,128)(2,1)} %bitcast.41, bf16[16,128,512]{2,1,0:T(8,128)(2,1)} %get-tuple-element.182, s32[]{:T(128)S(6)} %select_n.45), kind=kOutput, calls=%fused_computation.6.clone.1 | convolution fusion | flops 538968064 | bytes 6815748 | tf_op jit(solution)/shard_map/while/body/eval_jaxpr/jbvk,buk->jvbu/dot_general | solution.py:53
  127.3 2.0 copy.27
  130.0 1.0 constant_dynamic-slice_fusion.2
  131.0 1.6 shift_right_arithmetic.33
  132.6 2.9 %shift_right_arithmetic.34 = s32[8,128,4,128]{3,2,1,0:T(4,128)} reshape(s32[8,16,8,512]{3,2,1,0:T(8,128)} %shift_right_arithmetic.33) | data formatting | bytes 4194304 | tf_op jit(solution)/shard_map/while/body/eval_jaxpr/shift_right_arithmetic | solution.py:19
  135.6 2.6 fusion.29
  138.4 0.8 fusion.30
  139.2 1.1 constant_dynamic-update-slice_fusion.2
  141.7 2.8 %gather_fusion = bf16[32,128,512]{2,1,0:T(8,128)(2,1)} fusion(bf16[8,128,512]{2,1,0:T(8,128)(2,1)S(1)} %get-tuple-element.184, s32[1024]{0:T(1024)S(1)} %pad_clamp_fusion.2), kind=kCustom, calls=%fused_computation.clone.1 | custom fusion | bytes 8388736 | tf_op jit(solution)/shard_map/while/body/eval_jaxpr/gather | solution.py:49
  144.4 5.3 %divide_add_fusion.2 = f32[4,128,8,128]{3,1,2,0:T(8,128)} fusion(bf16[8,4,128,512]{3,2,1,0:T(8,128)(2,1)} %bitcast.41, bf16[16,128,512]{2,1,0:T(8,128)(2,1)} %get-tuple-element.182, s32[]{:T(128)S(6)} %select_n.45), kind=kOutput, calls=%fused_computation.6.clone.1 | convolution fusion | flops 538968064 | bytes 6815748 | tf_op jit(solution)/shard_map/while/body/eval_jaxpr/jbvk,buk->jvbu/dot_general | solution.py:53
  149.7 2.0 copy.27
  152.4 1.0 constant_dynamic-slice_fusion.2
  153.4 1.6 shift_right_arithmetic.33
  154.9 2.9 %shift_right_arithmetic.34 = s32[8,128,4,128]{3,2,1,0:T(4,128)} reshape(s32[8,16,8,512]{3,2,1,0:T(8,128)} %shift_right_arithmetic.33) | data formatting | bytes 4194304 | tf_op jit(solution)/shard_map/while/body/eval_jaxpr/shift_right_arithmetic | solution.py:19
  157.9 2.6 fusion.29
  160.8 0.8 fusion.30
  161.6 1.1 constant_dynamic-update-slice_fusion.2
  164.0 2.8 %gather_fusion = bf16[32,128,512]{2,1,0:T(8,128)(2,1)} fusion(bf16[8,128,512]{2,1,0:T(8,128)(2,1)S(1)} %get-tuple-element.184, s32[1024]{0:T(1024)S(1)} %pad_clamp_fusion.2), kind=kCustom, calls=%fused_computation.clone.1 | custom fusion | bytes 8388736 | tf_op jit(solution)/shard_map/while/body/eval_jaxpr/gather | solution.py:49
  166.8 5.3 %divide_add_fusion.2 = f32[4,128,8,128]{3,1,2,0:T(8,128)} fusion(bf16[8,4,128,512]{3,2,1,0:T(8,128)(2,1)} %bitcast.41, bf16[16,128,512]{2,1,0:T(8,128)(2,1)} %get-tuple-element.182, s32[]{:T(128)S(6)} %select_n.45), kind=kOutput, calls=%fused_computation.6.clone.1 | convolution fusion | flops 538968064 | bytes 6815748 | tf_op jit(solution)/shard_map/while/body/eval_jaxpr/jbvk,buk->jvbu/dot_general | solution.py:53
  172.0 2.0 copy.27
  174.7 1.0 constant_dynamic-slice_fusion.2
  175.7 1.6 shift_right_arithmetic.33
  177.3 2.9 %shift_right_arithmetic.34 = s32[8,128,4,128]{3,2,1,0:T(4,128)} reshape(s32[8,16,8,512]{3,2,1,0:T(8,128)} %shift_right_arithmetic.33) | data formatting | bytes 4194304 | tf_op jit(solution)/shard_map/while/body/eval_jaxpr/shift_right_arithmetic | solution.py:19
  180.3 2.6 fusion.29
  183.1 0.8 fusion.30
  183.9 1.1 constant_dynamic-update-slice_fusion.2
  185.0 1.0 copy-done.1
  186.1 43.4 %psum.7 = f32[512]{0:T(512)S(1)} all-reduce(f32[512]{0:T(512)S(1)} %convert_reduce_fusion), channel_id=1, replica_groups=mesh['row'=8,'col'=4] {'row','col'}, use_global_device_ids=true, to_apply=%region_4.5 | all-reduce | flops 512 | bytes 4096 | tf_op jit(solution)/shard_map/psum | solution.py:38
  229.5 32.2 %reduce-scatter.2.cloned.1.call-done = f32[512,512]{1,0:T(8,128)} async-done(((f32[2048,512]{1,0:T(8,128)}), f32[512,512]{1,0:T(8,128)}) %reduce-scatter.2.cloned.1.call-update) | async-done | bytes 1048592 | tf_op jit(solution)/shard_map/reduce_scatter | solution.py:64
  261.7 2.4 fusion.14
  (41 shorter events, 3.8 us)
Async XLA Ops:
  6.5 89.1 %copy-start.2 = (s32[1,8,16]{2,1,0:T(8,128)S(1)}, s32[1,8,16]{2,1,0:T(8,128)}, u32[]{:S(2)}) copy-start(s32[1,8,16]{2,1,0:T(8,128)} %param.8) | copy-start | bytes 1540
  6.5 42.0 %all-gather.5.cloned.1.call-start = ((), (), s32[]{:S(2)}) async-start(), calls=%async_computation.2 | async-start | bytes 4718592 | tf_op jit(solution)/shard_map/all_gather | solution.py:34
  7.3 88.4 %all-gather.3.cloned.1.call-start = ((), (), s32[]{:S(2)}) async-start(), calls=%async_computation.1 | async-start | bytes 2621440 | tf_op jit(solution)/shard_map/all_gather | solution.py:32
  8.0 253.7 %reduce-scatter.2.cloned.1.call-start = ((), (), s32[]{:S(2)}) async-start(), calls=%async_computation.3 | async-start | bytes 5242880 | tf_op jit(solution)/shard_map/reduce_scatter | solution.py:64
  113.3 2.8 %copy-start = (bf16[32,128,512]{2,1,0:T(8,128)(2,1)S(1)}, bf16[32,128,512]{2,1,0:T(8,128)(2,1)}, u32[]{:S(2)}) copy-start(bf16[32,128,512]{2,1,0:T(8,128)(2,1)} %gather_fusion) | copy-start | bytes 12582916 | tf_op jit(solution)/shard_map/while
  135.6 2.8 %copy-start = (bf16[32,128,512]{2,1,0:T(8,128)(2,1)S(1)}, bf16[32,128,512]{2,1,0:T(8,128)(2,1)}, u32[]{:S(2)}) copy-start(bf16[32,128,512]{2,1,0:T(8,128)(2,1)} %gather_fusion) | copy-start | bytes 12582916 | tf_op jit(solution)/shard_map/while
  157.9 2.8 %copy-start = (bf16[32,128,512]{2,1,0:T(8,128)(2,1)S(1)}, bf16[32,128,512]{2,1,0:T(8,128)(2,1)}, u32[]{:S(2)}) copy-start(bf16[32,128,512]{2,1,0:T(8,128)(2,1)} %gather_fusion) | copy-start | bytes 12582916 | tf_op jit(solution)/shard_map/while
  180.3 2.8 %copy-start = (bf16[32,128,512]{2,1,0:T(8,128)(2,1)S(1)}, bf16[32,128,512]{2,1,0:T(8,128)(2,1)}, u32[]{:S(2)}) copy-start(bf16[32,128,512]{2,1,0:T(8,128)(2,1)} %gather_fusion) | copy-start | bytes 12582916 | tf_op jit(solution)/shard_map/while
  185.0 1.0 copy-start.1
Sparse Core Ops, SparseCore 0:
  9.2 39.2 all-gather.4
  50.1 45.5 all-gather.2
  185.1 76.5 reduce-scatter.1
where the time goes:
time: 272 us; the launch traced here: 271 us
  waiting for transfers between devices  118 us (43%)
  local copies, waits for them, and re-layouts  52.9 us (19%)
  blocking collectives  43.4 us (16%)
  matrix products  24.2 us (9%)
  other arithmetic  14 us (5%)
  between operations  13.1 us (5%)
  loops' own time  5.22 us (2%)
    all_gather x1, waiting for transfers between devices, local(): range_rows = lax.all_gather(affiliation, 'col', axis=0, tiled=True)  44.3 us
    psum x1, blocking collectives, local(): lax.psum(jnp.sum(affiliation, axis=0, dtype=jnp.float32), ('row', 'col'))  43.4 us
    all_gather x1, waiting for transfers between devices, local(): group_rows = lax.all_gather(affiliation, 'row', axis=0, tiled=True)  39.8 us
    reduce_scatter x1, waiting for transfers between devices, local(): lax.psum_scatter(blocks_out.reshape(row_count, community), 'col', scatter...  32.2 us
    dot_general x4, matrix products, one_block(): jnp.einsum('jbvk,buk->jvbu', col_block, row_block, preferred_element_type...  21 us
    shift_right_arithmetic x16, local copies, waits for them, and re-layouts, unpack(): jnp.right_shift(mask_words[..., :, None, :], shifts[:, None])  18.3 us
    gather x4, local copies, waits for them, and re-layouts, one_block(): col_block = fetched[peer_ids]  11 us
    convert_element_type x4, other arithmetic, one_block(): (arc_bits * (1.0 / jnp.expm1(scores) + neg_weight)).astype(jnp.bfloat16)  10.5 us
  transfers between devices with their start and end apart: 3, of which 3 were waited for; matrix products, arithmetic and copies ran while one was open for 1% of the time, Pallas kernels for 0%

commit v1 on v0

--- a/solution.py
+++ b/solution.py
@@ -1,12 +1,16 @@
+import functools
 import math
 
 import jax
 import jax.numpy as jnp
 from jax import lax
+from jax.experimental import pallas as pl
+from jax.experimental.pallas import tpu as pltpu
 from jax.sharding import PartitionSpec as P
 
 TILE = 128
 NBR = 8
+MESH = pl.DeviceIdType.MESH
 
 
 BACKGROUND = 0.25
@@ -68,8 +72,262 @@
     gradient = merged - neg_weight * (column_sums[None, :] - own_values)
     return jnp.maximum(own_values + STEP_SIZE * gradient, 0.0)
 
+def step_kernel(
+    n_row, n_col, neg_weight,
+    peers_ref, wanted_ref, own_ref, words_ref, out_ref,
+    raw, stage, tiles, words_out, words_in, word_bits, weights, total,
+    note, notes, line_note, line_notes,
+    raw_send, raw_recv, tile_send, tile_recv, words_send, words_recv,
+    note_send, note_recv, line_send, line_recv,
+):
+    own_rows, community = own_ref.shape
+    own_tiles = own_rows // TILE
+    lanes = community // 128
+    p = lax.axis_index("row")
+    c = lax.axis_index("col")
+
+    def row_peer(k):
+        return lax.rem(p + k, n_row)
+
+    def col_peer(k):
+        return lax.rem(c + k, n_col)
+
+    def raw_copy(g, up):
+        target = jnp.clip(c + 1, 0, n_col - 1) if up else jnp.maximum(c - 1, 0)
+        return pltpu.make_async_remote_copy(
+            src_ref=raw.at[g], dst_ref=raw.at[g],
+            send_sem=raw_send.at[int(up), g], recv_sem=raw_recv.at[g],
+            device_id=(p, target), device_id_type=MESH)
+
+    def tile_copy(g, k, slot):
+        return pltpu.make_async_remote_copy(
+            src_ref=stage.at[g, k],
+            dst_ref=tiles.at[g, pl.ds(pl.multiple_of(slot * TILE, TILE), TILE)],
+            send_sem=tile_send.at[g, k], recv_sem=tile_recv.at[g, slot],
+            device_id=(row_peer(k), c), device_id_type=MESH)
+
+    def words_copy(k, slot):
+        return pltpu.make_async_remote_copy(
+            src_ref=words_out.at[k], dst_ref=words_in.at[slot],
+            send_sem=words_send.at[k], recv_sem=words_recv.at[slot],
+            device_id=(p, col_peer(k)), device_id_type=MESH)
+
+    def note_copy(k, slot):
+        return pltpu.make_async_remote_copy(
+            src_ref=note, dst_ref=notes.at[slot],
+            send_sem=note_send.at[k], recv_sem=note_recv.at[slot],
+            device_id=(row_peer(k), c), device_id_type=MESH)
+
+    def line_copy(k, slot):
+        return pltpu.make_async_remote_copy(
+            src_ref=line_note, dst_ref=line_notes.at[slot],
+            send_sem=line_send.at[k], recv_sem=line_recv.at[slot],
+            device_id=(p, col_peer(k)), device_id_type=MESH)
+
+    def each(first, last, body):
+        def step(i, carry):
+            body(i)
+            return carry
+        lax.fori_loop(first, last, step, 0)
+
+    barrier = pltpu.get_barrier_semaphore()
+    for k in range(1, n_row):
+        pl.semaphore_signal(barrier, inc=1, device_id=(row_peer(k), c), device_id_type=MESH)
+    for k in range(1, n_col):
+        pl.semaphore_signal(barrier, inc=1, device_id=(p, col_peer(k)), device_id_type=MESH)
+
+    raw[c] = own_ref[...]
+    total[...] = jnp.zeros_like(total)
+    sums = jnp.sum(own_ref[...].astype(jnp.float32), axis=0, keepdims=True)
+    note[...] = jnp.zeros_like(note)
+    note[pl.ds(0, n_row), :] = wanted_ref[...].astype(jnp.float32)
+    for i in range(lanes):
+        note[pl.ds(n_row + i, 1), :] = sums[:, i * 128:(i + 1) * 128]
+    notes[p] = note[...]
+    pl.semaphore_wait(barrier, n_row - 1 + n_col - 1)
+
+    each(1, n_row, lambda k: note_copy(k, p).start())
+    pl.when(c + 1 < n_col)(lambda: raw_copy(c, True).start())
+    pl.when(c > 0)(lambda: raw_copy(c, False).start())
+
+    def order_words(k):
+        b = col_peer(k)
+        for t in range(own_tiles):
+            at = b * own_tiles + t
+            lane = pl.ds(pl.multiple_of(at * TILE, TILE), TILE)
+            slot_words = [words_ref[j, :, lane] for j in range(NBR)]
+            slot_peer = [peers_ref[j, at] for j in range(NBR)]
+            for q in range(n_row):
+                got = jnp.zeros((TILE // 8, TILE), jnp.int32)
+                for j in range(NBR):
+                    got = jnp.where(slot_peer[j] == q, slot_words[j], got)
+                words_out[k, q * 16:(q + 1) * 16, t * TILE:(t + 1) * TILE] = (
+                    got.astype(jnp.float32).astype(jnp.bfloat16))
+
+    each(1, n_row, lambda k: note_copy(k, row_peer(k)).wait_recv())
+    line_note[...] = jnp.sum(notes[...], axis=0)
+    for r in range(n_row):
+        line_note[pl.ds(r, 1), :] = notes[r, pl.ds(p, 1), :]
+    line_notes[c] = line_note[...]
+    each(1, n_col, lambda k: line_copy(k, c).start())
+
+    def send_tiles(g):
+        def one(k):
+            r = row_peer(k)
+            wanted = line_notes[g, pl.ds(r, 1), :]
+            picks = [
+                jnp.broadcast_to(
+                    jnp.concatenate([jnp.where(wanted == i, 1.0, 0.0)] * lanes, axis=1),
+                    (16, community)).astype(jnp.bfloat16)
+                for i in range(own_tiles)]
+            for q in range(TILE // 16):
+                got = raw[g, q * 16:(q + 1) * 16, :] * picks[0]
+                for i in range(1, own_tiles):
+                    got = got + raw[g, i * TILE + q * 16:i * TILE + (q + 1) * 16, :] * picks[i]
+                stage[g, k, q * 16:(q + 1) * 16, :] = got
+
+        def send(k):
+            one(k)
+            tile_copy(g, k, p).start()
+
+        each(1, n_row, send)
+        one(0)
+        tiles[g, pl.ds(pl.multiple_of(p * TILE, TILE), TILE), :] = stage[g, 0]
+
+    chunk = math.gcd(4, n_row) * TILE
+    bit_of_row = lax.shift_left(1, lax.broadcasted_iota(jnp.int32, (chunk // 8, 8, own_rows), 1))
+    scale = math.log2(math.e)
+
+    def compute(g):
+        word_bits[...] = words_in[g].astype(jnp.float32).astype(jnp.int32)
+
+        def part(i):
+            rows = pl.ds(pl.multiple_of(i * chunk, chunk), chunk)
+            scores = lax.dot_general(
+                tiles[g, rows, :], own_ref[...], (((1,), (1,)), ((), ())),
+                preferred_element_type=jnp.float32)
+            grown = jnp.exp2(scores * (scale / community) + BACKGROUND * scale)
+            value = 1.0 / (grown - 1.0) + neg_weight
+            words = word_bits[pl.ds(pl.multiple_of(i * (chunk // 8), chunk // 8), chunk // 8), :]
+            arcs = jnp.bitwise_and(
+                jnp.broadcast_to(words[:, None, :], (chunk // 8, 8, own_rows)), bit_of_row)
+            value = jnp.where(arcs.reshape(chunk, own_rows) != 0, value, 0.0)
+            weights[rows, :] = value.astype(jnp.bfloat16)
+
+        each(0, n_row * TILE // chunk, part)
+        total[...] += lax.dot_general(
+            weights[...], tiles[g], (((0,), (0,)), ((), ())),
+            preferred_element_type=jnp.float32)
+
+    send_tiles(c)
+    each(0, n_col, order_words)
+    words_in[c] = words_out[0]
+    each(1, n_col, lambda k: words_copy(k, c).start())
+    each(1, n_col, lambda k: line_copy(k, col_peer(k)).wait_recv())
+
+    def sides(s, body):
+        @pl.when(c - s >= 0)
+        def _():
+            body(c - s, True)
+
+        @pl.when((s > 0) & (c + s < n_col))
+        def _():
+            body(c + s, False)
+
+    def arrive(g, up):
+        raw_copy(g, up).wait_recv()
+        if up:
+            pl.when(c + 1 < n_col)(lambda: raw_copy(g, True).start())
+        else:
+            pl.when(c > 0)(lambda: raw_copy(g, False).start())
+        send_tiles(g)
+
+    def use(g, up):
+        each(1, n_row, lambda k: tile_copy(g, k, row_peer(k)).wait_recv())
+        pl.when(g != c)(lambda: words_copy(1, g).wait_recv())
+        compute(g)
+
+    def step(s):
+        sides(s, arrive)
+        sides(s - 1, use)
+
+    each(1, n_col + 1, step)
+
+    sums_all = jnp.sum(line_notes[...], axis=0)
+    for i in range(lanes):
+        lane = slice(i * 128, (i + 1) * 128)
+        own_values = own_ref[:, lane].astype(jnp.float32)
+        gradient = total[:, lane] - neg_weight * (sums_all[n_row + i:n_row + i + 1, :] - own_values)
+        out_ref[:, lane] = jnp.maximum(own_values + STEP_SIZE * gradient, 0.0)
+
+    def sent(s):
+        def one(g, up):
+            if up:
+                pl.when(c + 1 < n_col)(lambda: raw_copy(g, True).wait_send())
+                pl.when((s == 0) & (c > 0))(lambda: raw_copy(g, False).wait_send())
+            else:
+                pl.when(c > 0)(lambda: raw_copy(g, False).wait_send())
+            each(1, n_row, lambda k: tile_copy(g, k, p).wait_send())
+        sides(s, one)
+
+    each(0, n_col, sent)
+    each(1, n_row, lambda k: note_copy(k, p).wait_send())
+    each(1, n_col, lambda k: line_copy(k, c).wait_send())
+    each(1, n_col, lambda k: words_copy(k, c).wait_send())
+
+
+def fused(n_row, n_col, affiliation, wanted_tiles, slot_peers, edge_words):
+    own_rows, community = affiliation.shape
+    neg_weight = NEG_RATE * NBR * TILE / (own_rows * n_row * n_col)
+    wanted = jnp.broadcast_to(wanted_tiles.reshape(n_row, 1), (n_row, 128))
+    peers = slot_peers.reshape(NBR, -1)
+    words = edge_words.reshape(NBR, TILE // 8, -1)
+    note_rows = -(-(n_row + community // 128) // 8) * 8
+    dense = n_row * TILE
+    dma = pltpu.SemaphoreType.DMA
+    vmem = pl.BlockSpec(memory_space=pltpu.VMEM)
+    return pl.pallas_call(
+        functools.partial(step_kernel, n_row, n_col, neg_weight),
+        out_shape=jax.ShapeDtypeStruct((own_rows, community), jnp.float32),
+        in_specs=[pl.BlockSpec(memory_space=pltpu.SMEM), vmem, vmem, vmem],
+        out_specs=vmem,
+        scratch_shapes=[
+            pltpu.VMEM((n_col, own_rows, community), jnp.bfloat16),
+            pltpu.VMEM((n_col, n_row, TILE, community), jnp.bfloat16),
+            pltpu.VMEM((n_col, dense, community), jnp.bfloat16),
+            pltpu.VMEM((n_col, dense // 8, own_rows), jnp.bfloat16),
+            pltpu.VMEM((n_col, dense // 8, own_rows), jnp.bfloat16),
+            pltpu.VMEM((dense // 8, own_rows), jnp.int32),
+            pltpu.VMEM((dense, own_rows), jnp.bfloat16),
+            pltpu.VMEM((own_rows, community), jnp.float32),
+            pltpu.VMEM((note_rows, 128), jnp.float32),
+            pltpu.VMEM((n_row, note_rows, 128), jnp.float32),
+            pltpu.VMEM((note_rows, 128), jnp.float32),
+            pltpu.VMEM((n_col, note_rows, 128), jnp.float32),
+            dma((2, n_col)), dma((n_col,)),
+            dma((n_col, n_row)), dma((n_col, n_row)),
+            dma((n_col,)), dma((n_col,)),
+            dma((n_row,)), dma((n_row,)),
+            dma((n_col,)), dma((n_col,)),
+        ],
+        compiler_params=pltpu.CompilerParams(
+            collective_id=0, has_side_effects=True, vmem_limit_bytes=56 * 2**20),
+    )(peers, wanted, affiliation, words)
+
+
+def fits(n_row, n_col, own_rows, community):
+    tile_bytes = 2 * TILE * community * 2 * n_row * n_col
+    return tile_bytes + 2 * own_rows * community * n_col < 16 * 2**20
+
 
 def solution(mesh):
+    n_row, n_col = mesh.shape["row"], mesh.shape["col"]
+
+    def part(affiliation, *rest):
+        if fits(n_row, n_col, *affiliation.shape):
+            return fused(n_row, n_col, affiliation, *rest)
+        return local(affiliation, *rest)
+
     in_specs = (
         P(("row", "col"), None),
         P("col", None, "row"),
@@ -77,4 +335,4 @@
         P("col", None, None, "row"),
     )
     out_specs = P(("row", "col"), None)
-    return jax.shard_map(local, mesh=mesh, in_specs=in_specs, out_specs=out_specs, check_vma=False)
+    return jax.shard_map(part, mesh=mesh, in_specs=in_specs, out_specs=out_specs, check_vma=False)

time: 272 us -> 75 us (0.28)
  waiting for transfers between devices: 118 us -> 0 us
  Pallas kernels: 0 us -> 71.2 us
  local copies, waits for them, and re-layouts: 52.9 us -> 3.58 us
  blocking collectives: 43.4 us -> 0 us
  matrix products: 24.2 us -> 0 us
  other arithmetic: 14 us -> 0 us
  between operations: 13.1 us -> 0.01 us
  loops' own time: 5.22 us -> 0 us
    all_gather x2 -> x0, waiting for transfers between devices: 84.1 us -> none  [the longest x1 44.3 us: local(): range_rows = lax.all_gather(affiliation, 'col', axis=0, tiled=True)]
    pallas_call x0 -> x1, Pallas kernels: none -> 71.2 us  [fused(): pl.pallas_call(functools.partial(step_kernel, n_row, n_col, neg_weight),...]
    psum x1 -> x0, blocking collectives: 43.4 us -> none  [local(): lax.psum(jnp.sum(affiliation, axis=0, dtype=jnp.float32), ('row', 'col'))]
    reduce_scatter x1 -> x0, waiting for transfers between devices: 32.2 us -> none  [local(): lax.psum_scatter(blocks_out.reshape(row_count, community), 'col', scatter...]
    dot_general x8 -> x0, matrix products: 24.2 us -> none  [the longest x4 21 us: one_block(): jnp.einsum('jbvk,buk->jvbu', col_block, row_block, preferred_element_type...]
    shift_right_arithmetic x16 -> x0, local copies, waits for them, and re-layouts: 18.3 us -> none  [unpack(): jnp.right_shift(mask_words[..., :, None, :], shifts[:, None])]
    gather x5 -> x0, local copies, waits for them, and re-layouts: 13.8 us -> none  [the longest x4 11 us: one_block(): col_block = fetched[peer_ids]]
    convert_element_type x4 -> x0, other arithmetic: 10.5 us -> none  [one_block(): (arc_bits * (1.0 / jnp.expm1(scores) + neg_weight)).astype(jnp.bfloat16)]
  transfers between devices with their start and end apart: 3 -> 0, of which waited for: 3 -> 0; matrix products, arithmetic and copies ran while one was open for 1% -> 0% of each run, Pallas kernels for 0% -> 0%
where the time goes in v1:
time: 75 us; the launch traced here: 74.8 us
  Pallas kernels  71.2 us (95%)
  local copies, waits for them, and re-layouts  3.58 us (5%)
    pallas_call x1, Pallas kernels, fused(): pl.pallas_call(functools.partial(step_kernel, n_row, n_col, neg_weight),...  71.2 us
    unnamed x3, local copies, waits for them, and re-layouts  2.92 us

profile of v1, /device:TPU:1, one launch (start us, length us, event | category | flops | bytes accessed | tf_op | source)
XLA Modules:
  0.0 74.8 jit_solution(7647854582848343291)
XLA Ops:
  0.0 0.0 copy-start
  0.0 0.7 copy-done
  0.7 0.7 broadcast_in_dim.8.wanted_ref
  1.3 71.2 %shard_map.46 = f32[512,512]{1,0:T(8,128)} custom-call(s32[8,16]{1,0:T(8,128)} %bitcast.4, s32[8,128]{1,0:T(8,128)} %broadcast_in_dim.8.wanted_ref, bf16[512,512]{1,0:T(8,128)(2,1)} %own_ref.1, s32[8,16,2048]{2,1,0:T(8,128)} %bitcast.3), custom_call_target="tpu_custom_call" | custom-call | tf_op jit(solution)/shard_map/pallas_call | solution.py:289
  72.6 2.3 %copy.6 = f32[512,512]{1,0:T(8,128)} copy(f32[512,512]{1,0:T(8,128)} %shard_map.46) | data formatting | bytes 2097152
Async XLA Ops:
  0.0 0.7 copy-start

commit v2 on v1

--- a/solution.py
+++ b/solution.py
@@ -10,6 +10,7 @@
 
 TILE = 128
 NBR = 8
+PIECES = 2
 MESH = pl.DeviceIdType.MESH
 
 
@@ -83,6 +84,7 @@
     own_rows, community = own_ref.shape
     own_tiles = own_rows // TILE
     lanes = community // 128
+    width = community // PIECES
     p = lax.axis_index("row")
     c = lax.axis_index("col")
 
@@ -92,18 +94,21 @@
     def col_peer(k):
         return lax.rem(c + k, n_col)
 
-    def raw_copy(g, up):
+    def piece(q):
+        return pl.ds(pl.multiple_of(q * width, width), width)
+
+    def raw_copy(g, up, q):
         target = jnp.clip(c + 1, 0, n_col - 1) if up else jnp.maximum(c - 1, 0)
         return pltpu.make_async_remote_copy(
-            src_ref=raw.at[g], dst_ref=raw.at[g],
-            send_sem=raw_send.at[int(up), g], recv_sem=raw_recv.at[g],
+            src_ref=raw.at[g, :, piece(q)], dst_ref=raw.at[g, :, piece(q)],
+            send_sem=raw_send.at[int(up), g, q], recv_sem=raw_recv.at[g, q],
             device_id=(p, target), device_id_type=MESH)
 
-    def tile_copy(g, k, slot):
-        return pltpu.make_async_remote_copy(
-            src_ref=stage.at[g, k],
-            dst_ref=tiles.at[g, pl.ds(pl.multiple_of(slot * TILE, TILE), TILE)],
-            send_sem=tile_send.at[g, k], recv_sem=tile_recv.at[g, slot],
+    def tile_copy(g, k, slot, q):
+        return pltpu.make_async_remote_copy(
+            src_ref=stage.at[g, k, :, piece(q)],
+            dst_ref=tiles.at[g, pl.ds(pl.multiple_of(slot * TILE, TILE), TILE), piece(q)],
+            send_sem=tile_send.at[g, q, k], recv_sem=tile_recv.at[g, q, slot],
             device_id=(row_peer(k), c), device_id_type=MESH)
 
     def words_copy(k, slot):
@@ -140,15 +145,19 @@
     total[...] = jnp.zeros_like(total)
     sums = jnp.sum(own_ref[...].astype(jnp.float32), axis=0, keepdims=True)
     note[...] = jnp.zeros_like(note)
-    note[pl.ds(0, n_row), :] = wanted_ref[...].astype(jnp.float32)
+    note[pl.ds(0, n_row), :] = jnp.broadcast_to(wanted_ref[...], (n_row, 128)).astype(jnp.float32)
     for i in range(lanes):
         note[pl.ds(n_row + i, 1), :] = sums[:, i * 128:(i + 1) * 128]
     notes[p] = note[...]
     pl.semaphore_wait(barrier, n_row - 1 + n_col - 1)
 
     each(1, n_row, lambda k: note_copy(k, p).start())
-    pl.when(c + 1 < n_col)(lambda: raw_copy(c, True).start())
-    pl.when(c > 0)(lambda: raw_copy(c, False).start())
+
+    def send_own(q):
+        pl.when(c + 1 < n_col)(lambda: raw_copy(c, True, q).start())
+        pl.when(c > 0)(lambda: raw_copy(c, False, q).start())
+
+    each(0, PIECES, send_own)
 
     def order_words(k):
         b = col_peer(k)
@@ -171,28 +180,28 @@
     line_notes[c] = line_note[...]
     each(1, n_col, lambda k: line_copy(k, c).start())
 
-    def send_tiles(g):
-        def one(k):
+    def send_tiles(g, q):
+        def pick(k):
             r = row_peer(k)
             wanted = line_notes[g, pl.ds(r, 1), :]
             picks = [
                 jnp.broadcast_to(
-                    jnp.concatenate([jnp.where(wanted == i, 1.0, 0.0)] * lanes, axis=1),
-                    (16, community)).astype(jnp.bfloat16)
+                    jnp.concatenate([jnp.where(wanted == i, 1.0, 0.0)] * (width // 128), axis=1),
+                    (16, width)).astype(jnp.bfloat16)
                 for i in range(own_tiles)]
-            for q in range(TILE // 16):
-                got = raw[g, q * 16:(q + 1) * 16, :] * picks[0]
+            for h in range(TILE // 16):
+                got = raw[g, h * 16:(h + 1) * 16, piece(q)] * picks[0]
                 for i in range(1, own_tiles):
-                    got = got + raw[g, i * TILE + q * 16:i * TILE + (q + 1) * 16, :] * picks[i]
-                stage[g, k, q * 16:(q + 1) * 16, :] = got
+                    got = got + raw[g, i * TILE + h * 16:i * TILE + (h + 1) * 16, piece(q)] * picks[i]
+                stage[g, k, h * 16:(h + 1) * 16, piece(q)] = got
 
         def send(k):
-            one(k)
-            tile_copy(g, k, p).start()
+            pick(k)
+            tile_copy(g, k, p, q).start()
 
         each(1, n_row, send)
-        one(0)
-        tiles[g, pl.ds(pl.multiple_of(p * TILE, TILE), TILE), :] = stage[g, 0]
+        pick(0)
+        tiles[g, pl.ds(pl.multiple_of(p * TILE, TILE), TILE), piece(q)] = stage[g, 0, :, piece(q)]
 
     chunk = math.gcd(4, n_row) * TILE
     bit_of_row = lax.shift_left(1, lax.broadcasted_iota(jnp.int32, (chunk // 8, 8, own_rows), 1))
@@ -219,7 +228,7 @@
             weights[...], tiles[g], (((0,), (0,)), ((), ())),
             preferred_element_type=jnp.float32)
 
-    send_tiles(c)
+    each(0, PIECES, lambda q: send_tiles(c, q))
     each(0, n_col, order_words)
     words_in[c] = words_out[0]
     each(1, n_col, lambda k: words_copy(k, c).start())
@@ -234,21 +243,22 @@
         def _():
             body(c + s, False)
 
-    def arrive(g, up):
-        raw_copy(g, up).wait_recv()
+    def arrive(g, up, q):
+        raw_copy(g, up, q).wait_recv()
         if up:
-            pl.when(c + 1 < n_col)(lambda: raw_copy(g, True).start())
+            pl.when(c + 1 < n_col)(lambda: raw_copy(g, True, q).start())
         else:
-            pl.when(c > 0)(lambda: raw_copy(g, False).start())
-        send_tiles(g)
+            pl.when(c > 0)(lambda: raw_copy(g, False, q).start())
+        send_tiles(g, q)
 
     def use(g, up):
-        each(1, n_row, lambda k: tile_copy(g, k, row_peer(k)).wait_recv())
+        each(0, PIECES, lambda q: each(
+            1, n_row, lambda k: tile_copy(g, k, row_peer(k), q).wait_recv()))
         pl.when(g != c)(lambda: words_copy(1, g).wait_recv())
         compute(g)
 
     def step(s):
-        sides(s, arrive)
+        each(0, PIECES, lambda q: sides(s, lambda g, up: arrive(g, up, q)))
         sides(s - 1, use)
 
     each(1, n_col + 1, step)
@@ -261,14 +271,14 @@
         out_ref[:, lane] = jnp.maximum(own_values + STEP_SIZE * gradient, 0.0)
 
     def sent(s):
-        def one(g, up):
+        def one(g, up, q):
             if up:
-                pl.when(c + 1 < n_col)(lambda: raw_copy(g, True).wait_send())
-                pl.when((s == 0) & (c > 0))(lambda: raw_copy(g, False).wait_send())
+                pl.when(c + 1 < n_col)(lambda: raw_copy(g, True, q).wait_send())
+                pl.when((s == 0) & (c > 0))(lambda: raw_copy(g, False, q).wait_send())
             else:
-                pl.when(c > 0)(lambda: raw_copy(g, False).wait_send())
-            each(1, n_row, lambda k: tile_copy(g, k, p).wait_send())
-        sides(s, one)
+                pl.when(c > 0)(lambda: raw_copy(g, False, q).wait_send())
+            each(1, n_row, lambda k: tile_copy(g, k, p, q).wait_send())
+        each(0, PIECES, lambda q: sides(s, lambda g, up: one(g, up, q)))
 
     each(0, n_col, sent)
     each(1, n_row, lambda k: note_copy(k, p).wait_send())
@@ -279,7 +289,7 @@
 def fused(n_row, n_col, affiliation, wanted_tiles, slot_peers, edge_words):
     own_rows, community = affiliation.shape
     neg_weight = NEG_RATE * NBR * TILE / (own_rows * n_row * n_col)
-    wanted = jnp.broadcast_to(wanted_tiles.reshape(n_row, 1), (n_row, 128))
+    wanted = wanted_tiles.reshape(n_row, 1)
     peers = slot_peers.reshape(NBR, -1)
     words = edge_words.reshape(NBR, TILE // 8, -1)
     note_rows = -(-(n_row + community // 128) // 8) * 8
@@ -304,8 +314,8 @@
             pltpu.VMEM((n_row, note_rows, 128), jnp.float32),
             pltpu.VMEM((note_rows, 128), jnp.float32),
             pltpu.VMEM((n_col, note_rows, 128), jnp.float32),
-            dma((2, n_col)), dma((n_col,)),
-            dma((n_col, n_row)), dma((n_col, n_row)),
+            dma((2, n_col, PIECES)), dma((n_col, PIECES)),
+            dma((n_col, PIECES, n_row)), dma((n_col, PIECES, n_row)),
             dma((n_col,)), dma((n_col,)),
             dma((n_row,)), dma((n_row,)),
             dma((n_col,)), dma((n_col,)),

time: 75 us -> 66.6 us (0.89)
  Pallas kernels: 71.2 us -> 62.8 us
    pallas_call x1, Pallas kernels: 71.2 us -> 62.8 us  [fused(): pl.pallas_call(functools.partial(step_kernel, n_row, n_col, neg_weight),...]
where the time goes in v2:
time: 66.6 us; the launch traced here: 66.4 us
  Pallas kernels  62.8 us (94%)
  local copies, waits for them, and re-layouts  3.59 us (5%)
    pallas_call x1, Pallas kernels, fused(): pl.pallas_call(functools.partial(step_kernel, n_row, n_col, neg_weight),...  62.8 us
    unnamed x3, local copies, waits for them, and re-layouts  2.92 us

profile of v2, /device:TPU:1, one launch (start us, length us, event | category | flops | bytes accessed | tf_op | source)
XLA Modules:
  0.0 66.4 jit_solution(6307323475218426733)
XLA Ops:
  0.0 0.0 copy-start
  0.0 0.7 copy-done
  0.7 0.7 %copy.5.wanted_ref = s32[8,1]{1,0:T(8,128)} copy(s32[8,1]{0,1:T(1,128)S(1)} %bitcast.5) | data formatting | bytes 64 | tf_op jit(solution)/shard_map/reshape | solution.py:292
  1.3 62.8 %shard_map.46 = f32[512,512]{1,0:T(8,128)} custom-call(s32[8,16]{1,0:T(8,128)} %bitcast.4, s32[8,1]{1,0:T(8,128)} %copy.5.wanted_ref, bf16[512,512]{1,0:T(8,128)(2,1)} %own_ref.1, s32[8,16,2048]{2,1,0:T(8,128)} %bitcast.3), custom_call_target="tpu_custom_call" | custom-call | tf_op jit(solution)/shard_map/pallas_call | solution.py:299
  64.2 2.3 %copy.7 = f32[512,512]{1,0:T(8,128)} copy(f32[512,512]{1,0:T(8,128)} %shard_map.46) | data formatting | bytes 2097152
Async XLA Ops:
  0.0 0.7 copy-start

commit v3 on v2

--- a/solution.py
+++ b/solution.py
@@ -89,25 +89,28 @@
     c = lax.axis_index("col")
 
     def row_peer(k):
-        return lax.rem(p + k, n_row)
+        far = lax.rem(n_row - k, n_row)
+        peer = 0
+        bit = 1
+        while bit < n_row:
+            peer = peer + lax.rem(lax.div(p, bit) + lax.div(far, bit), 2) * bit
+            bit *= 2
+        return peer
 
     def col_peer(k):
         return lax.rem(c + k, n_col)
 
-    def piece(q):
-        return pl.ds(pl.multiple_of(q * width, width), width)
-
     def raw_copy(g, up, q):
         target = jnp.clip(c + 1, 0, n_col - 1) if up else jnp.maximum(c - 1, 0)
         return pltpu.make_async_remote_copy(
-            src_ref=raw.at[g, :, piece(q)], dst_ref=raw.at[g, :, piece(q)],
+            src_ref=raw.at[g, q], dst_ref=raw.at[g, q],
             send_sem=raw_send.at[int(up), g, q], recv_sem=raw_recv.at[g, q],
             device_id=(p, target), device_id_type=MESH)
 
     def tile_copy(g, k, slot, q):
         return pltpu.make_async_remote_copy(
-            src_ref=stage.at[g, k, :, piece(q)],
-            dst_ref=tiles.at[g, pl.ds(pl.multiple_of(slot * TILE, TILE), TILE), piece(q)],
+            src_ref=stage.at[g, q, k],
+            dst_ref=tiles.at[g, q, pl.ds(pl.multiple_of(slot * TILE, TILE), TILE)],
             send_sem=tile_send.at[g, q, k], recv_sem=tile_recv.at[g, q, slot],
             device_id=(row_peer(k), c), device_id_type=MESH)
 
@@ -141,7 +144,8 @@
     for k in range(1, n_col):
         pl.semaphore_signal(barrier, inc=1, device_id=(p, col_peer(k)), device_id_type=MESH)
 
-    raw[c] = own_ref[...]
+    for q in range(PIECES):
+        raw[c, q] = own_ref[:, q * width:(q + 1) * width]
     total[...] = jnp.zeros_like(total)
     sums = jnp.sum(own_ref[...].astype(jnp.float32), axis=0, keepdims=True)
     note[...] = jnp.zeros_like(note)
@@ -190,10 +194,10 @@
                     (16, width)).astype(jnp.bfloat16)
                 for i in range(own_tiles)]
             for h in range(TILE // 16):
-                got = raw[g, h * 16:(h + 1) * 16, piece(q)] * picks[0]
+                got = raw[g, q, h * 16:(h + 1) * 16, :] * picks[0]
                 for i in range(1, own_tiles):
-                    got = got + raw[g, i * TILE + h * 16:i * TILE + (h + 1) * 16, piece(q)] * picks[i]
-                stage[g, k, h * 16:(h + 1) * 16, piece(q)] = got
+                    got = got + raw[g, q, i * TILE + h * 16:i * TILE + (h + 1) * 16, :] * picks[i]
+                stage[g, q, k, h * 16:(h + 1) * 16, :] = got
 
         def send(k):
             pick(k)
@@ -201,7 +205,7 @@
 
         each(1, n_row, send)
         pick(0)
-        tiles[g, pl.ds(pl.multiple_of(p * TILE, TILE), TILE), piece(q)] = stage[g, 0, :, piece(q)]
+        tiles[g, q, pl.ds(pl.multiple_of(p * TILE, TILE), TILE), :] = stage[g, q, 0]
 
     chunk = math.gcd(4, n_row) * TILE
     bit_of_row = lax.shift_left(1, lax.broadcasted_iota(jnp.int32, (chunk // 8, 8, own_rows), 1))
@@ -212,9 +216,11 @@
 
         def part(i):
             rows = pl.ds(pl.multiple_of(i * chunk, chunk), chunk)
-            scores = lax.dot_general(
-                tiles[g, rows, :], own_ref[...], (((1,), (1,)), ((), ())),
-                preferred_element_type=jnp.float32)
+            scores = sum(
+                lax.dot_general(
+                    tiles[g, q, rows, :], raw[c, q], (((1,), (1,)), ((), ())),
+                    preferred_element_type=jnp.float32)
+                for q in range(PIECES))
             grown = jnp.exp2(scores * (scale / community) + BACKGROUND * scale)
             value = 1.0 / (grown - 1.0) + neg_weight
             words = word_bits[pl.ds(pl.multiple_of(i * (chunk // 8), chunk // 8), chunk // 8), :]
@@ -224,9 +230,10 @@
             weights[rows, :] = value.astype(jnp.bfloat16)
 
         each(0, n_row * TILE // chunk, part)
-        total[...] += lax.dot_general(
-            weights[...], tiles[g], (((0,), (0,)), ((), ())),
-            preferred_element_type=jnp.float32)
+        for q in range(PIECES):
+            total[:, q * width:(q + 1) * width] += lax.dot_general(
+                weights[...], tiles[g, q], (((0,), (0,)), ((), ())),
+                preferred_element_type=jnp.float32)
 
     each(0, PIECES, lambda q: send_tiles(c, q))
     each(0, n_col, order_words)
@@ -294,6 +301,7 @@
     words = edge_words.reshape(NBR, TILE // 8, -1)
     note_rows = -(-(n_row + community // 128) // 8) * 8
     dense = n_row * TILE
+    width = community // PIECES
     dma = pltpu.SemaphoreType.DMA
     vmem = pl.BlockSpec(memory_space=pltpu.VMEM)
     return pl.pallas_call(
@@ -302,9 +310,9 @@
         in_specs=[pl.BlockSpec(memory_space=pltpu.SMEM), vmem, vmem, vmem],
         out_specs=vmem,
         scratch_shapes=[
-            pltpu.VMEM((n_col, own_rows, community), jnp.bfloat16),
-            pltpu.VMEM((n_col, n_row, TILE, community), jnp.bfloat16),
-            pltpu.VMEM((n_col, dense, community), jnp.bfloat16),
+            pltpu.VMEM((n_col, PIECES, own_rows, width), jnp.bfloat16),
+            pltpu.VMEM((n_col, PIECES, n_row, TILE, width), jnp.bfloat16),
+            pltpu.VMEM((n_col, PIECES, dense, width), jnp.bfloat16),
             pltpu.VMEM((n_col, dense // 8, own_rows), jnp.bfloat16),
             pltpu.VMEM((n_col, dense // 8, own_rows), jnp.bfloat16),
             pltpu.VMEM((dense // 8, own_rows), jnp.int32),
@@ -327,7 +335,7 @@
 
 def fits(n_row, n_col, own_rows, community):
     tile_bytes = 2 * TILE * community * 2 * n_row * n_col
-    return tile_bytes + 2 * own_rows * community * n_col < 16 * 2**20
+    return n_row & (n_row - 1) == 0 and tile_bytes + 2 * own_rows * community * n_col < 16 * 2**20
 
 
 def solution(mesh):

time: 66.6 us -> 67.3 us (1.011); the launches traced: 66.4 us -> 66.1 us
  no operation moved by 1% of the time
where the time goes in v3:
time: 67.3 us; the launch traced here: 66.1 us
  Pallas kernels  62.5 us (93%)
  local copies, waits for them, and re-layouts  3.59 us (5%)
    pallas_call x1, Pallas kernels, fused(): pl.pallas_call(functools.partial(step_kernel, n_row, n_col, neg_weight),...  62.5 us
    unnamed x3, local copies, waits for them, and re-layouts  2.92 us

profile of v3, /device:TPU:1, one launch (start us, length us, event | category | flops | bytes accessed | tf_op | source)
XLA Modules:
  0.0 66.1 jit_solution(104552458044488765)
XLA Ops:
  0.0 0.0 copy-start
  0.0 0.7 copy-done
  0.7 0.7 %copy.5.wanted_ref = s32[8,1]{1,0:T(8,128)} copy(s32[8,1]{0,1:T(1,128)S(1)} %bitcast.5) | data formatting | bytes 64 | tf_op jit(solution)/shard_map/reshape | solution.py:299
  1.3 62.5 %shard_map.46 = f32[512,512]{1,0:T(8,128)} custom-call(s32[8,16]{1,0:T(8,128)} %bitcast.4, s32[8,1]{1,0:T(8,128)} %copy.5.wanted_ref, bf16[512,512]{1,0:T(8,128)(2,1)} %own_ref.1, s32[8,16,2048]{2,1,0:T(8,128)} %bitcast.3), custom_call_target="tpu_custom_call" | custom-call | tf_op jit(solution)/shard_map/pallas_call | solution.py:307
  63.8 2.3 %copy.7 = f32[512,512]{1,0:T(8,128)} copy(f32[512,512]{1,0:T(8,128)} %shard_map.46) | data formatting | bytes 2097152
Async XLA Ops:
  0.0 0.7 copy-start

commit v4 on v2

--- a/solution.py
+++ b/solution.py
@@ -75,7 +75,7 @@
 
 def step_kernel(
     n_row, n_col, neg_weight,
-    peers_ref, wanted_ref, own_ref, words_ref, out_ref,
+    peers_ref, wanted_ref, own_ref, words_hbm, out_ref, words_ref, words_sem,
     raw, stage, tiles, words_out, words_in, word_bits, weights, total,
     note, notes, line_note, line_notes,
     raw_send, raw_recv, tile_send, tile_recv, words_send, words_recv,
@@ -135,6 +135,8 @@
             return carry
         lax.fori_loop(first, last, step, 0)
 
+    words_fetch = pltpu.make_async_copy(words_hbm, words_ref, words_sem)
+    words_fetch.start()
     barrier = pltpu.get_barrier_semaphore()
     for k in range(1, n_row):
         pl.semaphore_signal(barrier, inc=1, device_id=(row_peer(k), c), device_id_type=MESH)
@@ -145,7 +147,8 @@
     total[...] = jnp.zeros_like(total)
     sums = jnp.sum(own_ref[...].astype(jnp.float32), axis=0, keepdims=True)
     note[...] = jnp.zeros_like(note)
-    note[pl.ds(0, n_row), :] = jnp.broadcast_to(wanted_ref[...], (n_row, 128)).astype(jnp.float32)
+    for i in range(n_row):
+        note[pl.ds(i, 1), :] = jnp.full((1, 128), wanted_ref[i], jnp.int32).astype(jnp.float32)
     for i in range(lanes):
         note[pl.ds(n_row + i, 1), :] = sums[:, i * 128:(i + 1) * 128]
     notes[p] = note[...]
@@ -229,6 +232,7 @@
             preferred_element_type=jnp.float32)
 
     each(0, PIECES, lambda q: send_tiles(c, q))
+    words_fetch.wait()
     each(0, n_col, order_words)
     words_in[c] = words_out[0]
     each(1, n_col, lambda k: words_copy(k, c).start())
@@ -268,7 +272,7 @@
         lane = slice(i * 128, (i + 1) * 128)
         own_values = own_ref[:, lane].astype(jnp.float32)
         gradient = total[:, lane] - neg_weight * (sums_all[n_row + i:n_row + i + 1, :] - own_values)
-        out_ref[:, lane] = jnp.maximum(own_values + STEP_SIZE * gradient, 0.0)
+        out_ref[:, lane] = own_values + STEP_SIZE * gradient
 
     def sent(s):
         def one(g, up, q):
@@ -289,19 +293,21 @@
 def fused(n_row, n_col, affiliation, wanted_tiles, slot_peers, edge_words):
     own_rows, community = affiliation.shape
     neg_weight = NEG_RATE * NBR * TILE / (own_rows * n_row * n_col)
-    wanted = wanted_tiles.reshape(n_row, 1)
+    wanted = wanted_tiles.reshape(n_row)
     peers = slot_peers.reshape(NBR, -1)
     words = edge_words.reshape(NBR, TILE // 8, -1)
     note_rows = -(-(n_row + community // 128) // 8) * 8
     dense = n_row * TILE
     dma = pltpu.SemaphoreType.DMA
     vmem = pl.BlockSpec(memory_space=pltpu.VMEM)
-    return pl.pallas_call(
+    smem = pl.BlockSpec(memory_space=pltpu.SMEM)
+    moved = pl.pallas_call(
         functools.partial(step_kernel, n_row, n_col, neg_weight),
         out_shape=jax.ShapeDtypeStruct((own_rows, community), jnp.float32),
-        in_specs=[pl.BlockSpec(memory_space=pltpu.SMEM), vmem, vmem, vmem],
+        in_specs=[smem, smem, vmem, pl.BlockSpec(memory_space=pl.ANY)],
         out_specs=vmem,
         scratch_shapes=[
+            pltpu.VMEM(words.shape, jnp.int32), dma,
             pltpu.VMEM((n_col, own_rows, community), jnp.bfloat16),
             pltpu.VMEM((n_col, n_row, TILE, community), jnp.bfloat16),
             pltpu.VMEM((n_col, dense, community), jnp.bfloat16),
@@ -323,6 +329,7 @@
         compiler_params=pltpu.CompilerParams(
             collective_id=0, has_side_effects=True, vmem_limit_bytes=56 * 2**20),
     )(peers, wanted, affiliation, words)
+    return jnp.maximum(moved, 0.0)
 
 
 def fits(n_row, n_col, own_rows, community):

time: 66.6 us -> 64.9 us (0.974)
  local copies, waits for them, and re-layouts: 3.59 us -> 0 us
  other arithmetic: 0 us -> 2.29 us
    unnamed x3 -> x0, local copies, waits for them, and re-layouts: 2.92 us -> none
    max x0 -> x1, other arithmetic: none -> 2.29 us  [fused(): return jnp.maximum(moved, 0.0)]
    reshape x1 -> x0, local copies, waits for them, and re-layouts: 0.67 us -> none  [fused(): wanted = wanted_tiles.reshape(n_row, 1)]
where the time goes in v4:
time: 64.9 us; the launch traced here: 64.7 us
  Pallas kernels  62.4 us (96%)
  other arithmetic  2.29 us (4%)
    pallas_call x1, Pallas kernels, fused(): pl.pallas_call(functools.partial(step_kernel, n_row, n_col, neg_weight),...  62.4 us
    max x1, other arithmetic, fused(): return jnp.maximum(moved, 0.0)  2.29 us

profile of v4, /device:TPU:1, one launch (start us, length us, event | category | flops | bytes accessed | tf_op | source)
XLA Modules:
  0.0 64.7 jit_solution(8481684960771766641)
XLA Ops:
  0.0 62.4 %shard_map.46 = f32[512,512]{1,0:T(8,128)} custom-call(s32[8,16]{1,0:T(8,128)} %bitcast.4, s32[8]{0:T(128)} %bitcast.5, bf16[512,512]{1,0:T(8,128)(2,1)} %own_ref.1, s32[8,16,2048]{2,1,0:T(8,128)} %bitcast.3), custom_call_target="tpu_custom_call" | custom-call | tf_op jit(solution)/shard_map/pallas_call | solution.py:304
  62.5 2.3 %broadcast_maximum_fusion = f32[512,512]{1,0:T(8,128)} fusion(f32[512,512]{1,0:T(8,128)} %shard_map.46), kind=kLoop, calls=%fused_computation | loop fusion | flops 262144 | bytes 2097152 | tf_op jit(solution)/shard_map/max | solution.py:332

commit v5 on v4

--- a/solution.py
+++ b/solution.py
@@ -207,13 +207,19 @@
         tiles[g, pl.ds(pl.multiple_of(p * TILE, TILE), TILE), piece(q)] = stage[g, 0, :, piece(q)]
 
     chunk = math.gcd(4, n_row) * TILE
+    parts = n_row * TILE // chunk
     bit_of_row = lax.shift_left(1, lax.broadcasted_iota(jnp.int32, (chunk // 8, 8, own_rows), 1))
     scale = math.log2(math.e)
 
     def compute(g):
         word_bits[...] = words_in[g].astype(jnp.float32).astype(jnp.int32)
 
-        def part(i):
+        def part(step):
+            i = lax.rem(lax.div(p, chunk // TILE) + step, parts)
+            for j in range(chunk // TILE):
+                slot = i * (chunk // TILE) + j
+                pl.when(slot != p)(lambda slot=slot: each(
+                    0, PIECES, lambda q: tile_copy(g, 1, slot, q).wait_recv()))
             rows = pl.ds(pl.multiple_of(i * chunk, chunk), chunk)
             scores = lax.dot_general(
                 tiles[g, rows, :], own_ref[...], (((1,), (1,)), ((), ())),
@@ -226,7 +232,7 @@
             value = jnp.where(arcs.reshape(chunk, own_rows) != 0, value, 0.0)
             weights[rows, :] = value.astype(jnp.bfloat16)
 
-        each(0, n_row * TILE // chunk, part)
+        each(0, parts, part)
         total[...] += lax.dot_general(
             weights[...], tiles[g], (((0,), (0,)), ((), ())),
             preferred_element_type=jnp.float32)
@@ -256,8 +262,6 @@
         send_tiles(g, q)
 
     def use(g, up):
-        each(0, PIECES, lambda q: each(
-            1, n_row, lambda k: tile_copy(g, k, row_peer(k), q).wait_recv()))
         pl.when(g != c)(lambda: words_copy(1, g).wait_recv())
         compute(g)
 

time: 64.9 us -> 65 us (level)
  no operation moved by 1% of the time
where the time goes in v5:
time: 65 us; the launch traced here: 64.8 us
  Pallas kernels  62.5 us (96%)
  other arithmetic  2.29 us (4%)
    pallas_call x1, Pallas kernels, fused(): pl.pallas_call(functools.partial(step_kernel, n_row, n_col, neg_weight),...  62.5 us
    max x1, other arithmetic, fused(): return jnp.maximum(moved, 0.0)  2.29 us

profile of v5, /device:TPU:1, one launch (start us, length us, event | category | flops | bytes accessed | tf_op | source)
XLA Modules:
  0.0 64.8 jit_solution(13690663777203073286)
XLA Ops:
  0.0 62.5 %shard_map.46 = f32[512,512]{1,0:T(8,128)} custom-call(s32[8,16]{1,0:T(8,128)} %bitcast.4, s32[8]{0:T(128)} %bitcast.5, bf16[512,512]{1,0:T(8,128)(2,1)} %own_ref.1, s32[8,16,2048]{2,1,0:T(8,128)} %bitcast.3), custom_call_target="tpu_custom_call" | custom-call | tf_op jit(solution)/shard_map/pallas_call | solution.py:308
  62.5 2.3 %broadcast_maximum_fusion = f32[512,512]{1,0:T(8,128)} fusion(f32[512,512]{1,0:T(8,128)} %shard_map.46), kind=kLoop, calls=%fused_computation | loop fusion | flops 262144 | bytes 2097152 | tf_op jit(solution)/shard_map/max | solution.py:336
